TPU v7x, 32 devices: a whole 2x2x4 slice. The times are simulated.
32 devices in a mesh: dp: 4 (over y, x), tensor: 8 (over z, core).
Axes of the slice: x: 2, y: 2, z: 4, core: 2. Of those that a mesh axis runs over, the one named last changes fastest.
Arguments:
- tokens: bfloat16 [65536, 1024], P(('dp', 'tensor')), may hold values from -6 to 6
- routes: int32 [32, 256], P(('dp', 'tensor')), may hold values from 0 to 2047, as said below
- router_weight: bfloat16 [1024], replicated, may hold values from -0.1875 to 0.1875
- attn_gain: float32 [1024], replicated, may hold values from 0.5 to 1.5
- qkv_weight: bfloat16 [3, 16, 64, 1024], P(None, 'tensor'), may hold values from -0.1875 to 0.1875
- out_weight: bfloat16 [16, 64, 1024], P('tensor'), may hold values from -1 to 1
- mlp_gain: float32 [1024], replicated, may hold values from 0.5 to 1.5
- up_weight: bfloat16 [1024, 4096], P(None, 'tensor'), may hold values from -0.1875 to 0.1875
- down_weight: bfloat16 [4096, 1024], P('tensor'), may hold values from -0.09375 to 0.09375
- cotangent: bfloat16 [65536, 1024], P(('dp', 'tensor')), may hold values from -6 to 6
Outputs:
- output: bfloat16 [65536, 1024], P(('dp', 'tensor'))
- tokens_grad: bfloat16 [65536, 1024], P(('dp', 'tensor'))
- router_grad: float32 [1024], replicated
- attn_gain_grad: float32 [1024], replicated
- qkv_grad: float32 [3, 16, 64, 1024], P(None, 'tensor')
- out_grad: float32 [16, 64, 1024], P('tensor')
- mlp_gain_grad: float32 [1024], replicated
- up_grad: float32 [1024, 4096], P(None, 'tensor')
- down_grad: float32 [4096, 1024], P('tensor')
Inputs may be any that keep to these rules, and one draw needn't show every extreme that they name: `routes`: each row lists 256 different token positions of one sequence in increasing order; the first and the last position of every sequence are always listed.
All inputs are finite; a program needn't handle non-finite values.
Results may differ from a plain program's by a relative error of at most 0.019.
Values may be sent and summed in bfloat16 or wider, within the bound.
No kernel may reach another device: no remote copies, remote signals or barrier semaphores. Data moves between devices by JAX's collectives and lax.ppermute only.
A program may use at most 256 MiB of HBM per device.

v0:
```python
from functools import partial

import jax
import jax.numpy as jnp
from jax import lax
from jax.sharding import PartitionSpec as P

epsilon = 1e-05


def normalize(values, gain):
    inverse = lax.rsqrt(jnp.mean(values * values, axis=1, keepdims=True) + epsilon)
    return values * inverse * gain


def norm_back(values, gain, upstream):
    inverse = lax.rsqrt(jnp.mean(values * values, axis=1, keepdims=True) + epsilon)
    unit_rows = values * inverse
    scaled = upstream * gain
    values_grad = inverse * (
        scaled - unit_rows * jnp.mean(scaled * unit_rows, axis=1, keepdims=True)
    )
    return (values_grad, jnp.sum(upstream * unit_rows, axis=0))


def scores_of(query_heads, key_heads):
    scaling = query_heads.shape[3] ** (-0.5)
    logits = (
        jnp.einsum("hnqe,hnke->hnqk", query_heads, key_heads, preferred_element_type=jnp.float32)
        * scaling
    )
    positions = jnp.arange(query_heads.shape[2])
    allowed = positions[:, None] >= positions[None, :]
    return jnp.where(allowed, logits, -1e30)


def attend(query_heads, key_heads, value_heads):
    logits = scores_of(query_heads, key_heads)
    highest_score = jnp.max(logits, axis=3, keepdims=True)
    log_total = highest_score + jnp.log(
        jnp.sum(jnp.exp(logits - highest_score), axis=3, keepdims=True)
    )
    softmaxed = jnp.exp(logits - log_total)
    attended = jnp.einsum(
        "hnqk,hnke->hnqe",
        softmaxed.astype(jnp.bfloat16),
        value_heads,
        preferred_element_type=jnp.float32,
    )
    return (attended.astype(jnp.bfloat16), log_total)


def attend_back(query_heads, key_heads, value_heads, log_total, attended_grad):
    logits = scores_of(query_heads, key_heads)
    softmaxed = jnp.exp(logits - log_total)
    value_grad = jnp.einsum(
        "hnqk,hnqe->hnke",
        softmaxed.astype(jnp.bfloat16),
        attended_grad,
        preferred_element_type=jnp.float32,
    )
    prob_grad = jnp.einsum(
        "hnqe,hnke->hnqk", attended_grad, value_heads, preferred_element_type=jnp.float32
    )
    logit_grad = (
        softmaxed * (prob_grad - jnp.sum(softmaxed * prob_grad, axis=3, keepdims=True))
    ).astype(jnp.bfloat16)
    scaling = query_heads.shape[3] ** (-0.5)
    query_grad = (
        jnp.einsum("hnqk,hnke->hnqe", logit_grad, key_heads, preferred_element_type=jnp.float32)
        * scaling
    )
    key_grad = (
        jnp.einsum("hnqk,hnqe->hnke", logit_grad, query_heads, preferred_element_type=jnp.float32)
        * scaling
    )
    return (query_grad, key_grad, value_grad)


def row_product(source_rows, weight_mat):
    return jnp.dot(source_rows, weight_mat, preferred_element_type=jnp.float32)


def row_product_back(source_rows, weight_mat):
    return lax.dot_general(
        source_rows, weight_mat, (((1,), (1,)), ((), ())), preferred_element_type=jnp.float32
    )


def head_product(proj_grad, weight_mat):
    return jnp.einsum("chge,ched->gd", proj_grad, weight_mat, preferred_element_type=jnp.float32)


def local(
    tokens,
    routes,
    router_weight,
    attn_gain,
    qkv_weight,
    out_weight,
    mlp_gain,
    up_weight,
    down_weight,
    cotangent,
):
    seq_count = routes.shape[0]
    count_routed = routes.shape[1]
    model_width = tokens.shape[1]
    length = tokens.shape[0] // seq_count
    own_rows = seq_count * count_routed
    picker = (jnp.arange(seq_count)[:, None], routes)
    token_seqs = tokens.reshape(seq_count, length, model_width)
    grad_seqs = cotangent.reshape(seq_count, length, model_width)
    routed_rows = token_seqs[picker].reshape(own_rows, model_width)
    grad_rows = grad_seqs[picker].reshape(own_rows, model_width).astype(jnp.float32)
    rows_wide = routed_rows.astype(jnp.float32)
    router_score = jnp.dot(routed_rows, router_weight, preferred_element_type=jnp.float32)
    qkv_w, out_w, up_w, down_w = (qkv_weight, out_weight, up_weight, down_weight)
    group_rows = lax.all_gather(routed_rows, "tensor", axis=0, tiled=True)
    start_own = lax.axis_index("tensor") * own_rows
    heads_local = qkv_w.shape[1]
    head_size = qkv_w.shape[2]
    total_rows = group_rows.shape[0]
    group_seqs = total_rows // count_routed
    group_wide = group_rows.astype(jnp.float32)
    normed_in = normalize(group_wide, attn_gain).astype(jnp.bfloat16)
    projected = jnp.einsum(
        "gd,ched->chge", normed_in, qkv_w, preferred_element_type=jnp.float32
    ).astype(jnp.bfloat16)
    projected = projected.reshape(3, heads_local, group_seqs, count_routed, head_size)
    query_heads = projected[0]
    key_heads = projected[1]
    value_heads = projected[2]
    attended, log_total = attend(query_heads, key_heads, value_heads)
    attended_rows = attended.transpose(1, 2, 0, 3).reshape(total_rows, heads_local * head_size)
    out_flat = out_w.reshape(heads_local * head_size, model_width)
    attn_all = lax.psum(
        jnp.dot(attended_rows, out_flat, preferred_element_type=jnp.float32).astype(jnp.bfloat16),
        "tensor",
    ).astype(jnp.float32)
    mixed_all = group_wide + attn_all
    normed_group = normalize(mixed_all, mlp_gain).astype(jnp.bfloat16)
    attn_own = lax.dynamic_slice_in_dim(attn_all, start_own, own_rows, 0)
    mixed_own = lax.dynamic_slice_in_dim(mixed_all, start_own, own_rows, 0)
    pre_act = jnp.dot(normed_group, up_w, preferred_element_type=jnp.float32)
    hidden = jax.nn.gelu(pre_act, approximate=True).astype(jnp.bfloat16)
    mlp_own = lax.psum_scatter(
        row_product(hidden, down_w).astype(jnp.bfloat16), "tensor", scatter_dimension=0, tiled=True
    ).astype(jnp.float32)
    branch_sum = attn_own + mlp_own
    result_rows = (rows_wide + router_score[:, None] * branch_sum).astype(jnp.bfloat16)
    output = (
        token_seqs.at[picker]
        .set(result_rows.reshape(seq_count, count_routed, model_width))
        .reshape(tokens.shape)
    )
    branch_term = grad_rows * router_score[:, None]
    score_grad = jnp.sum(grad_rows * branch_sum, axis=1)
    branch_low = branch_term.astype(jnp.bfloat16)
    branch_group = lax.all_gather(branch_low, "tensor", axis=0, tiled=True)
    hidden_grad = lax.dot_general(
        branch_group, down_w, (((1,), (1,)), ((), ())), preferred_element_type=jnp.float32
    )
    down_grad = lax.dot_general(
        hidden, branch_group, (((0,), (0,)), ((), ())), preferred_element_type=jnp.float32
    )
    gelu_value, gelu_back = jax.vjp(partial(jax.nn.gelu, approximate=True), pre_act)
    pre_grad = gelu_back(hidden_grad)[0].astype(jnp.bfloat16)
    up_grad = lax.dot_general(
        normed_group, pre_grad, (((0,), (0,)), ((), ())), preferred_element_type=jnp.float32
    )
    mid_grad = lax.psum_scatter(
        row_product_back(pre_grad, up_w).astype(jnp.bfloat16),
        "tensor",
        scatter_dimension=0,
        tiled=True,
    ).astype(jnp.float32)
    mixed_grad, mlp_gain_part = norm_back(mixed_own, mlp_gain, mid_grad)
    attn_low = (branch_term + mixed_grad).astype(jnp.bfloat16)
    attn_group = lax.all_gather(attn_low, "tensor", axis=0, tiled=True)
    attended_grad = lax.dot_general(
        attn_group, out_flat, (((1,), (1,)), ((), ())), preferred_element_type=jnp.float32
    ).astype(jnp.bfloat16)
    out_grad = lax.dot_general(
        attended_rows, attn_group, (((0,), (0,)), ((), ())), preferred_element_type=jnp.float32
    )
    out_grad = out_grad.reshape(heads_local, head_size, model_width)
    attended_grad = attended_grad.reshape(
        group_seqs, count_routed, heads_local, head_size
    ).transpose(2, 0, 1, 3)
    query_grad, key_grad, value_grad = attend_back(
        query_heads, key_heads, value_heads, log_total, attended_grad
    )
    proj_grad = (
        jnp.stack([query_grad, key_grad, value_grad])
        .astype(jnp.bfloat16)
        .reshape(3, heads_local, total_rows, head_size)
    )
    qkv_grad = jnp.einsum("chge,gd->ched", proj_grad, normed_in, preferred_element_type=jnp.float32)
    normed_grad = lax.psum_scatter(
        head_product(proj_grad, qkv_w).astype(jnp.bfloat16),
        "tensor",
        scatter_dimension=0,
        tiled=True,
    ).astype(jnp.float32)
    rows_back, attn_gain_part = norm_back(rows_wide, attn_gain, normed_grad)
    rows_total = grad_rows + (
        mixed_grad + rows_back + score_grad[:, None] * router_weight.astype(jnp.float32)
    )
    tokens_grad = (
        grad_seqs.at[picker]
        .set(rows_total.astype(jnp.bfloat16).reshape(seq_count, count_routed, model_width))
        .reshape(cotangent.shape)
    )
    router_part = jnp.dot(score_grad, rows_wide, precision=lax.Precision.HIGHEST)
    qkv_grad, out_grad, up_grad, down_grad = (
        lax.psum(qkv_grad.astype(jnp.bfloat16), "dp").astype(jnp.float32),
        lax.psum(out_grad.astype(jnp.bfloat16), "dp").astype(jnp.float32),
        lax.psum(up_grad.astype(jnp.bfloat16), "dp").astype(jnp.float32),
        lax.psum(down_grad.astype(jnp.bfloat16), "dp").astype(jnp.float32),
    )
    router_grad, attn_gain_grad, mlp_gain_grad = lax.psum(
        (router_part, attn_gain_part, mlp_gain_part), ("dp", "tensor")
    )
    return (
        output,
        tokens_grad,
        router_grad,
        attn_gain_grad,
        qkv_grad,
        out_grad,
        mlp_gain_grad,
        up_grad,
        down_grad,
    )


def solution(mesh):
    return jax.shard_map(
        local,
        mesh=mesh,
        in_specs=(
            P(("dp", "tensor"), None),
            P(("dp", "tensor"), None),
            P(),
            P(),
            P(None, "tensor", None, None),
            P("tensor", None, None),
            P(),
            P(None, "tensor"),
            P("tensor", None),
            P(("dp", "tensor"), None),
        ),
        out_specs=(
            P(("dp", "tensor"), None),
            P(("dp", "tensor"), None),
            P(),
            P(),
            P(None, "tensor", None, None),
            P("tensor", None, None),
            P(),
            P(None, "tensor"),
            P("tensor", None),
        ),
        check_vma=False,
    )
```

profile of v0, /device:TPU:0, one launch (start us, length us, event | category | flops | bytes accessed | tf_op | source)
XLA Modules:
  0.0 607.3 jit_solution(1503833714954388818)
XLA Ops:
  7.2 4.8 copy.93
  14.1 4.0 gather_fusion
  23.4 44.8 %all-gather.9.cloned.1.call-done = bf16[2048,1024]{1,0:T(8,128)(2,1)} async-done(((bf16[256,1024]{1,0:T(8,128)(2,1)}), bf16[2048,1024]{1,0:T(8,128)(2,1)}) %all-gather.9.cloned.1.call-update) | async-done | bytes 4194320 | tf_op jit(solution)/shard_map/all_gather | solution.py:119
  82.5 33.8 %all-gather.5.cloned.1.call-done = bf16[2048,1024]{1,0:T(8,128)(2,1)} async-done(((bf16[256,1024]{1,0:T(8,128)(2,1)}), bf16[2048,1024]{1,0:T(8,128)(2,1)}) %all-gather.5.cloned.1.call-update) | async-done | bytes 4194320 | tf_op jit(solution)/shard_map/all_gather | solution.py:160
  116.3 6.8 %fusion.80 = f32[2048,512]{1,0:T(8,128)} fusion(bf16[2048,1024]{1,0:T(8,128)(2,1)} %all-gather.5.cloned.1.call-done, bf16[512,1024]{1,0:T(8,128)(2,1)} %param.18), kind=kOutput, calls=%fused_computation.125 | convolution fusion | flops 2147483648 | bytes 9437184 | tf_op jit(solution)/shard_map/dot_general | solution.py:161
  123.1 90.7 %all-reduce.6.cloned.1.call-done = bf16[2048,1024]{1,0:T(8,128)(2,1)} async-done(((bf16[2048,1024]{1,0:T(8,128)(2,1)}), bf16[2048,1024]{1,0:T(8,128)(2,1)}) %all-reduce.6.cloned.1.call-update) | async-done | bytes 4194320 | tf_op jit(solution)/shard_map/psum | solution.py:137
  213.9 9.1 %convert_add_fusion = (f32[2048,1024]{1,0:T(8,128)}, f32[2048]{0:T(1024)S(1)}) fusion(bf16[2048,1024]{1,0:T(8,128)(2,1)} %all-gather.9.cloned.1.call-done, bf16[2048,1024]{1,0:T(8,128)(2,1)} %all-reduce.6.cloned.1.call-done), kind=kLoop, calls=%fused_computation.4 | loop fusion | flops 10483712 | bytes 16785408 | tf_op jit(solution)/shard_map/add | solution.py:141
  223.8 6.7 %fusion.9 = (bf16[2048,512]{1,0:T(8,128)(2,1)S(1)}, f32[2048,512]{1,0:T(8,128)}) fusion(f32[2048,512]{1,0:T(8,128)S(1)} %copy-done.27, bf16[1024,512]{1,0:T(8,128)(2,1)S(1)} %copy-done, f32[1024]{0:T(1024)S(1)} %copy-done.21, f32[2048]{0:T(1024)S(1)} %add_rsqrt_fusion, bf16[2048,1024]{1,0:T(8,128)(2,1)S(1)} %copy-done.5, bf16[2048,1024]{1,0:T(8,128)(2,1)S(1)} %copy-done.8), kind=kOutput, calls=%fused_computation.21 | convolution fusion | flops 2181038080 | bytes 19935232 | tf_op jit(solution)/shard_map/dot_general | solution.py:145
  231.8 4.4 convolution_convert_fusion
  237.4 6.9 %convolution_convert_fusion.1 = bf16[2048,1024]{1,0:T(8,128)(2,1)} fusion(bf16[512,1024]{1,0:T(8,128)(2,1)S(1)} %copy-done.25, f32[2048,512]{1,0:T(8,128)} %get-tuple-element.32), kind=kOutput, calls=%fused_computation.32 | convolution fusion | flops 2159017984 | bytes 9437184 | tf_op jit(solution)/shard_map/dot_general | solution.py:81
  244.4 6.5 %convert_element_type.121 = f32[2048,1024]{1,0:T(8,128)} convert(bf16[2048,1024]{1,0:T(8,128)(2,1)} %all-reduce.6.cloned.1.call-done) | non-fusion elementwise | flops 2097152 | bytes 12582912 | tf_op jit(solution)/shard_map/convert_element_type | solution.py:140
  252.3 34.2 %reduce-scatter.6.cloned.1.call-done = bf16[256,1024]{1,0:T(8,128)(2,1)} async-done(((bf16[2048,1024]{1,0:T(8,128)(2,1)}), bf16[256,1024]{1,0:T(8,128)(2,1)}) %reduce-scatter.6.cloned.1.call-update) | async-done | bytes 524304 | tf_op jit(solution)/shard_map/reduce_scatter | solution.py:172
  288.3 48.5 %reduce-scatter.4.cloned.1.call-done = bf16[256,1024]{1,0:T(8,128)(2,1)} async-done(((bf16[2048,1024]{1,0:T(8,128)(2,1)}), bf16[256,1024]{1,0:T(8,128)(2,1)}) %reduce-scatter.4.cloned.1.call-update) | async-done | bytes 524304 | tf_op jit(solution)/shard_map/reduce_scatter | solution.py:147
  340.3 7.0 %convolution_convert_fusion.5 = bf16[512,1024]{1,0:T(8,128)(2,1)} fusion(bf16[2048,1024]{1,0:T(8,128)(2,1)} %all-gather.5.cloned.1.call-done, f32[2048,512]{1,0:T(8,128)} %get-tuple-element.32), kind=kOutput, calls=%fused_computation.46 | convolution fusion | flops 2157445120 | bytes 9437184 | tf_op jit(solution)/shard_map/dot_general | solution.py:164
  347.4 4.1 convolution_convert_fusion.6
  351.5 34.0 %all-gather.7.cloned.1.call-done = bf16[2048,1024]{1,0:T(8,128)(2,1)} async-done(((bf16[256,1024]{1,0:T(8,128)(2,1)}), bf16[2048,1024]{1,0:T(8,128)(2,1)}) %all-gather.7.cloned.1.call-update) | async-done | bytes 4194320 | tf_op jit(solution)/shard_map/all_gather | solution.py:180
  391.2 3.5 convolution_convert_fusion.8
  406.3 4.2 fusion.33
  413.5 5.9 bitcast_convert_fusion
  420.5 7.4 %scatter_custom_fusion = bf16[2048,1024]{1,0:T(8,128)(2,1)} fusion(bf16[2048,1024]{1,0:T(8,128)(2,1)} %copy.93, s32[256]{0:T(256)S(1)} %bitcast.133, bf16[256,1024]{1,0:T(8,128)(2,1)S(1)} %copy-done.4, bf16[256,1024]{1,0:T(8,128)(2,1)S(1)} %copy-done.13, f32[2048,1024]{1,0:T(8,128)} %convert_element_type.121, s32[]{:T(128)S(6)} %select_n.17, ...), kind=kCustom, calls=%fused_computation.85 | custom fusion | flops 1572864 | bytes 6292996 | tf_op jit(solution)/shard_map/scatter | solution.py:154
  428.2 72.0 %all-reduce.8.cloned.1.call-done = (bf16[3,2,64,1024]{3,2,1,0:T(8,128)(2,1)}, bf16[2,64,1024]{2,1,0:T(8,128)(2,1)}, bf16[1024,512]{1,0:T(8,128)(2,1)}, bf16[512,1024]{1,0:T(8,128)(2,1)}) async-done(((bf16[3,2,64,1024]{3,2,1,0:T(8,128)(2,1)}, bf16[2,64,1024]{2,1,0:T(8,128)(2,1)}, bf16[1024,512]{1,0:T(8,128)(2,1)}, bf16[512,1024]{1,0:T(8,128)(2,1)}), (bf16[3,2,64,1024]{3,2,1,0:T(8,128)(2,1)}, ...) | async-done | bytes 3145744 | tf_op jit(solution)/shard_map/psum | solution.py:217
  508.9 43.6 %reduce-scatter.8.cloned.1.call-done = bf16[256,1024]{1,0:T(8,128)(2,1)} async-done(((bf16[2048,1024]{1,0:T(8,128)(2,1)}), bf16[256,1024]{1,0:T(8,128)(2,1)}) %reduce-scatter.8.cloned.1.call-update) | async-done | bytes 524304 | tf_op jit(solution)/shard_map/reduce_scatter | solution.py:200
  554.1 38.2 %all-reduce.1 = (f32[1024]{0:T(1024)}, f32[1024]{0:T(1024)}, f32[1024]{0:T(1024)}) all-reduce(f32[1024]{0:T(1024)S(1)} %bitcast.131, f32[1024]{0:T(1024)S(1)} %get-tuple-element.11, f32[1024]{0:T(1024)S(1)} %get-tuple-element.9), channel_id=1, replica_groups=mesh['dp'=4,'tensor'=8] {'dp','tensor'}, use_global_device_ids=true, to_apply=%region_16.17 | all-reduce | flops 3072 | bytes 24576 | tf_op jit(solution)/shard_map/psum | solution.py:222
  592.3 8.0 %scatter_custom_fusion.1 = bf16[2048,1024]{1,0:T(8,128)(2,1)} fusion(bf16[2048,1024]{1,0:T(8,128)(2,1)} %copy.94, s32[256]{0:T(256)S(1)} %bitcast.134, bf16[256,1024]{1,0:T(8,128)(2,1)S(1)} %copy-done.4, bf16[256,1024]{1,0:T(8,128)(2,1)} %reduce-scatter.8.cloned.1.call-done, bf16[256,1024]{1,0:T(8,128)(2,1)S(1)} %gather_fusion.1, ...), kind=kCustom, calls=%fused_computation.84 | custom fusion | flops 4980736 | bytes 7357444 | tf_op jit(solution)/shard_map/scatter | solution.py:212
  (132 shorter events, 63.3 us)
Async XLA Ops:
  7.2 215.8 %copy-start = (bf16[1024,512]{1,0:T(8,128)(2,1)S(1)}, bf16[1024,512]{1,0:T(8,128)(2,1)}, u32[]{:S(2)}) copy-start(bf16[1024,512]{1,0:T(8,128)(2,1)} %param.17) | copy-start | bytes 3145732
  7.2 61.0 %all-gather.9.cloned.1.call-start = ((), (), s32[]{:S(2)}) async-start(), calls=%async_computation.9 | async-start | bytes 4718592 | tf_op jit(solution)/shard_map/all_gather | solution.py:119
  7.2 4.8 copy-start.12
  18.2 98.1 %all-gather.5.cloned.1.call-start = ((), (), s32[]{:S(2)}) async-start(), calls=%async_computation.5 | async-start | bytes 4718592 | tf_op jit(solution)/shard_map/all_gather | solution.py:160
  21.5 49.9 %copy-start.22 = (f32[1024]{0:T(1024)S(1)}, f32[1024]{0:T(1024)}, u32[]{:S(2)}) copy-start(f32[1024]{0:T(1024)} %param.13) | copy-start | bytes 12292
  22.7 191.1 %all-reduce.6.cloned.1.call-start = ((), (), s32[]{:S(2)}) async-start(), calls=%async_computation.3 | async-start | bytes 8388608 | tf_op jit(solution)/shard_map/psum | solution.py:137
  82.3 204.2 %reduce-scatter.6.cloned.1.call-start = ((), (), s32[]{:S(2)}) async-start(), calls=%async_computation.6 | async-start | bytes 4718592 | tf_op jit(solution)/shard_map/reduce_scatter | solution.py:172
  123.1 99.9 %copy-start.21 = (f32[1024]{0:T(1024)S(1)}, f32[1024]{0:T(1024)}, u32[]{:S(2)}) copy-start(f32[1024]{0:T(1024)} %param.16) | copy-start | bytes 12292
  213.9 9.1 %copy-start.5 = (bf16[2048,1024]{1,0:T(8,128)(2,1)S(1)}, bf16[2048,1024]{1,0:T(8,128)(2,1)}, u32[]{:S(2)}) copy-start(bf16[2048,1024]{1,0:T(8,128)(2,1)} %all-reduce.6.cloned.1.call-done) | copy-start | bytes 12582916
  213.9 9.1 %copy-start.8 = (bf16[2048,1024]{1,0:T(8,128)(2,1)S(1)}, bf16[2048,1024]{1,0:T(8,128)(2,1)}, u32[]{:S(2)}) copy-start(bf16[2048,1024]{1,0:T(8,128)(2,1)} %all-gather.9.cloned.1.call-done) | copy-start | bytes 12582916
  213.9 9.9 %copy-start.27 = (f32[2048,512]{1,0:T(8,128)S(1)}, f32[2048,512]{1,0:T(8,128)}, u32[]{:S(2)}) copy-start(f32[2048,512]{1,0:T(8,128)} %fusion.80) | copy-start | bytes 12582916
  236.2 100.6 %reduce-scatter.4.cloned.1.call-start = ((), (), s32[]{:S(2)}) async-start(), calls=%async_computation.4 | async-start | bytes 4718592 | tf_op jit(solution)/shard_map/reduce_scatter | solution.py:147
  244.3 141.1 %all-gather.7.cloned.1.call-start = ((), (), s32[]{:S(2)}) async-start(), calls=%async_computation.7 | async-start | bytes 4718592 | tf_op jit(solution)/shard_map/all_gather | solution.py:180
  340.0 160.1 %all-reduce.8.cloned.1.call-start = ((), (), s32[]{:S(2)}) async-start(), calls=%async_computation.10 | async-start | bytes 6291456 | tf_op jit(solution)/shard_map/psum | solution.py:217
  340.3 7.1 %copy-start.6 = (bf16[2048,1024]{1,0:T(8,128)(2,1)S(1)}, bf16[2048,1024]{1,0:T(8,128)(2,1)}, u32[]{:S(2)}) copy-start(bf16[2048,1024]{1,0:T(8,128)(2,1)} %all-reduce.6.cloned.1.call-done) | copy-start | bytes 12582916
  340.3 7.1 %copy-start.9 = (bf16[2048,1024]{1,0:T(8,128)(2,1)S(1)}, bf16[2048,1024]{1,0:T(8,128)(2,1)}, u32[]{:S(2)}) copy-start(bf16[2048,1024]{1,0:T(8,128)(2,1)} %all-gather.9.cloned.1.call-done) | copy-start | bytes 12582916
  340.3 7.1 %copy-start.29 = (bf16[2048,512]{1,0:T(8,128)(2,1)S(1)}, bf16[2048,512]{1,0:T(8,128)(2,1)}, u32[]{:S(2)}) copy-start(bf16[2048,512]{1,0:T(8,128)(2,1)} %copy-done.28) | copy-start | bytes 6291460
  389.9 4.9 copy-start.3
  389.9 4.9 copy-start.15
  406.2 4.4 copy-start.10
  413.5 139.1 %reduce-scatter.8.cloned.1.call-start = ((), (), s32[]{:S(2)}) async-start(), calls=%async_computation.8 | async-start | bytes 4718592 | tf_op jit(solution)/shard_map/reduce_scatter | solution.py:200
  500.1 7.2 %copy-start.18 = (bf16[512,1024]{1,0:T(8,128)(2,1)S(1)}, bf16[512,1024]{1,0:T(8,128)(2,1)}, u32[]{:S(2)}) copy-start(bf16[512,1024]{1,0:T(8,128)(2,1)} %get-tuple-element.19) | copy-start | bytes 3145732
  504.5 87.8 %copy-start.11 = (bf16[256,1024]{1,0:T(8,128)(2,1)S(1)}, bf16[256,1024]{1,0:T(8,128)(2,1)}, u32[]{:S(2)}) copy-start(bf16[256,1024]{1,0:T(8,128)(2,1)} %reduce-scatter.6.cloned.1.call-done) | copy-start | bytes 1572868
  507.4 92.9 %copy-start.1 = (bf16[1024,512]{1,0:T(8,128)(2,1)S(1)}, bf16[1024,512]{1,0:T(8,128)(2,1)}, u32[]{:S(2)}) copy-start(bf16[1024,512]{1,0:T(8,128)(2,1)} %param.17) | copy-start | bytes 3145732
  (14 other events, 31.8 us)
Sparse Core Ops, SparseCore 0:
  18.3 49.8 all-gather.8
  70.4 45.9 all-gather.4
  118.7 95.1 all-reduce.5
  236.4 50.0 reduce-scatter.5
  288.6 48.1 reduce-scatter.3
  340.1 45.2 all-gather.6
  413.6 86.4 all-reduce.7
  502.5 49.9 reduce-scatter.7
where the time goes:
time: 613 us; the launch traced here: 607 us
  waiting for transfers between devices  402 us (66%)
  matrix products  68.9 us (11%)
  other arithmetic  54.2 us (9%)
  blocking collectives  38.2 us (6%)
  local copies, waits for them, and re-layouts  28.2 us (5%)
  between operations  14.8 us (2%)
    psum x1, waiting for transfers between devices, local(): lax.psum(jnp.dot(attended_rows, out_flat, preferred_element_type=jnp.floa...  90.7 us
    psum x1, waiting for transfers between devices, local(): lax.psum(qkv_grad.astype(jnp.bfloat16), 'dp').astype(jnp.float32)  72 us
    reduce_scatter x1, waiting for transfers between devices, local(): lax.psum_scatter(row_product(hidden, down_w).astype(jnp.bfloat16), 'tenso...  48.5 us
    all_gather x1, waiting for transfers between devices, local(): group_rows = lax.all_gather(routed_rows, 'tensor', axis=0, tiled=True)  44.8 us
    reduce_scatter x1, waiting for transfers between devices, local(): lax.psum_scatter(head_product(proj_grad, qkv_w).astype(jnp.bfloat16), 'te...  43.6 us
    psum x1, blocking collectives, local(): lax.psum((router_part, attn_gain_part, mlp_gain_part), ('dp', 'tensor'))  38.2 us
    reduce_scatter x1, waiting for transfers between devices, local(): lax.psum_scatter(row_product_back(pre_grad, up_w).astype(jnp.bfloat16), '...  34.2 us
    all_gather x1, waiting for transfers between devices, local(): attn_group = lax.all_gather(attn_low, 'tensor', axis=0, tiled=True)  34 us
  transfers between devices with their start and end apart: 8, of which 8 were waited for; matrix products, arithmetic and copies ran while one was open for 12% of the time, Pallas kernels for 0%

commit v1 on v0

v1 whole, which is shorter than its diff:
```python
import jax
import jax.numpy as jnp
from jax import lax
from jax.sharding import PartitionSpec as P

epsilon = 1e-05
f32 = jnp.float32
low = jnp.bfloat16


def inverse_rms(values):
    return lax.rsqrt(jnp.mean(values * values, axis=1, keepdims=True) + epsilon)


def norm_back(values, inverse, gain, upstream):
    unit_rows = values * inverse
    scaled = upstream * gain
    return inverse * (scaled - unit_rows * jnp.mean(scaled * unit_rows, axis=1, keepdims=True))


def dot(a, b, contract):
    return lax.dot_general(a, b, (contract, ((), ())), preferred_element_type=f32)


def make_local(dp_size, tensor_size):
    dp_bits = [1 << k for k in range(dp_size.bit_length() - 1)]
    far_bits = [1 << k for k in range(2, tensor_size.bit_length() - 1)]

    def swap(x, axis, bit):
        size = dp_size if axis == "dp" else tensor_size
        return lax.ppermute(x, axis, [(i, i ^ bit) for i in range(size)])

    def gather_rows(x):
        near = swap(x, "tensor", 2)
        core = swap(x, "tensor", 1)
        both = swap(near, "tensor", 1)
        return jnp.concatenate([x, near, core, both], axis=0)

    def scatter_rows(keep, send):
        rows = keep.shape[0] // 2
        near = keep[rows:] + swap(send[rows:], "tensor", 1).astype(f32)
        own = keep[:rows] + swap(send[:rows], "tensor", 1).astype(f32)
        return own + swap(near.astype(low), "tensor", 2).astype(f32)

    def product_scatter(left, weight, contract):
        half = left.shape[0] // 2
        send = dot(left[half:], weight, contract).astype(low)
        keep = dot(left[:half], weight, contract)
        return scatter_rows(keep, send)

    def spread(own, axis, order):
        me = lax.axis_index("dp")
        size = own.shape[axis] // dp_size
        mine = [
            lax.dynamic_slice_in_dim(own, (me ^ r) * size, size, axis) for r in range(dp_size)
        ]
        shards = [mine[0]]
        for bit in far_bits:
            shards = shards + [swap(s, "tensor", bit) for s in shards]
        found = [mine]
        for shard in shards[1:]:
            pieces = {0: shard}
            for bit in order:
                pieces.update({r ^ bit: swap(p, "dp", bit) for r, p in pieces.items()})
            found.append([pieces[r] for r in range(dp_size)])
        return found

    def collect(grad, order):
        me = lax.axis_index("dp")
        held = {r: grad[:, r] for r in range(dp_size)}
        for bit in order:
            sent = [r for r in held if r & bit]
            came = swap(jnp.stack([held[r] for r in sent]), "dp", bit)
            held = {
                r ^ bit: (held[r ^ bit].astype(f32) + came[k].astype(f32)).astype(low)
                for k, r in enumerate(sent)
            }
        total = held[0]
        for bit in reversed(far_bits):
            half = total.shape[0] // 2
            came = swap(total[half:], "tensor", bit)
            total = (total[:half].astype(f32) + came.astype(f32)).astype(low)
        pieces = {0: total[0]}
        for bit in reversed(order):
            pieces.update({r ^ bit: swap(p, "dp", bit) for r, p in pieces.items()})
        stacked = jnp.stack([pieces[r] for r in range(dp_size)])
        return jnp.concatenate(
            [lax.dynamic_slice_in_dim(stacked, me ^ a, 1, 0) for a in range(dp_size)], axis=0
        ).astype(f32)

    def local(
        tokens,
        routes,
        router_weight,
        attn_gain,
        qkv_weight,
        out_weight,
        mlp_gain,
        up_weight,
        down_weight,
        cotangent,
    ):
        seq_count, routed = routes.shape
        width = tokens.shape[1]
        length = tokens.shape[0] // seq_count
        own_rows = seq_count * routed
        heads, head_size = qkv_weight.shape[1:3]
        hidden_own = up_weight.shape[1]

        places = (routes + jnp.arange(seq_count, dtype=jnp.int32)[:, None] * length).reshape(own_rows)
        token_ids = jnp.arange(tokens.shape[0], dtype=jnp.int32)
        chosen = (places[:, None] == token_ids[None, :]).astype(low)
        rows = dot(chosen, tokens, ((1,), (0,)))
        grad_rows = dot(chosen, cotangent, ((1,), (0,)))

        first, second = dp_bits, dp_bits[::-1]
        qkv_all = jnp.concatenate(
            [p for s in spread(qkv_weight.reshape(3, heads, head_size, width), 2, first) for p in [jnp.concatenate(s, axis=2)]],
            axis=1,
        )
        out_all = jnp.concatenate([jnp.concatenate(s, axis=1) for s in spread(out_weight, 1, second)], axis=0)
        up_all = jnp.concatenate([p for s in spread(up_weight, 1, first) for p in s], axis=1)
        down_all = jnp.concatenate([p for s in spread(down_weight, 0, second) for p in s], axis=0)
        all_heads = qkv_all.shape[1]
        shard_count = all_heads // heads
        qkv_flat = qkv_all.reshape(3 * all_heads * head_size, width)
        out_flat = out_all.reshape(all_heads * head_size, width)

        score = jnp.sum(rows * router_weight.astype(f32), axis=1, keepdims=True)
        inverse_in = inverse_rms(rows)
        normed_in = gather_rows((rows * inverse_in * attn_gain).astype(low))
        branch_term = grad_rows * score
        branch = gather_rows(branch_term.astype(low))

        group_rows = normed_in.shape[0]
        group_seqs = group_rows // routed
        projected = dot(qkv_flat, normed_in, ((1,), (1,))).astype(low)
        projected = projected.reshape(3, all_heads, head_size, group_seqs, routed)
        query, key, value = projected[0], projected[1], projected[2]
        scaling = head_size**-0.5
        order = jnp.arange(routed)
        logits = jnp.einsum("heni,henj->hnij", query, key, preferred_element_type=f32) * scaling
        logits = jnp.where(order[:, None] >= order[None, :], logits, -1e30)
        highest = jnp.max(logits, axis=3, keepdims=True)
        exponent = jnp.exp(logits - highest)
        softmaxed = exponent / jnp.sum(exponent, axis=3, keepdims=True)
        probs_low = softmaxed.astype(low)
        attended = jnp.einsum("hnij,henj->heni", probs_low, value, preferred_element_type=f32)
        attended = attended.astype(low).reshape(all_heads * head_size, group_rows)
        attended_rows = attended.T
        attn_sum = product_scatter(attended_rows, out_flat, ((1,), (0,)))
        mixed = rows + attn_sum
        inverse_mid = inverse_rms(mixed)
        normed_mid = gather_rows((mixed * inverse_mid * mlp_gain).astype(low))

        pre_act = dot(normed_mid, up_all, ((1,), (0,)))
        inner = jnp.sqrt(2 / jnp.pi).astype(f32) * (pre_act + 0.044715 * pre_act**3)
        tanh = jnp.tanh(inner)
        hidden = (0.5 * pre_act * (1 + tanh)).astype(low)
        slope = 0.5 * (1 + tanh) + 0.5 * pre_act * (1 - tanh * tanh) * jnp.sqrt(2 / jnp.pi).astype(f32) * (
            1 + 3 * 0.044715 * pre_act * pre_act
        )
        hidden_grad = dot(branch, down_all, ((1,), (1,)))
        pre_grad = (hidden_grad * slope).astype(low)
        mid_grad = product_scatter(pre_grad, up_all, ((1,), (1,)))
        mlp_sum = product_scatter(hidden, down_all, ((1,), (0,)))
        down_grad = dot(hidden, branch, ((0,), (0,)))
        up_grad = dot(pre_grad, normed_mid, ((0,), (0,)))
        mlp_gain_part = jnp.sum(up_all.astype(f32).T * up_grad, axis=0) / mlp_gain

        mixed_grad = norm_back(mixed, inverse_mid, mlp_gain, mid_grad)
        attn_grad = gather_rows((branch_term + mixed_grad).astype(low))
        attended_grad = dot(out_flat, attn_grad, ((1,), (1,))).astype(low)
        out_grad = dot(attended, attn_grad, ((1,), (0,)))
        attended_grad = attended_grad.reshape(all_heads, head_size, group_seqs, routed)
        value_grad = jnp.einsum("hnij,heni->henj", probs_low, attended_grad, preferred_element_type=f32)
        prob_grad = jnp.einsum("heni,henj->hnij", attended_grad, value, preferred_element_type=f32)
        logit_grad = (
            softmaxed * (prob_grad - jnp.sum(softmaxed * prob_grad, axis=3, keepdims=True))
        ).astype(low)
        query_grad = jnp.einsum("hnij,henj->heni", logit_grad, key, preferred_element_type=f32) * scaling
        key_grad = jnp.einsum("hnij,heni->henj", logit_grad, query, preferred_element_type=f32) * scaling
        proj_grad = jnp.stack([query_grad, key_grad, value_grad]).astype(low)
        proj_grad = proj_grad.reshape(3 * all_heads * head_size, group_rows)
        qkv_grad = dot(proj_grad, normed_in, ((1,), (0,)))
        normed_grad = product_scatter(proj_grad.T, qkv_flat, ((1,), (0,)))
        attn_gain_part = jnp.sum(qkv_flat.astype(f32) * qkv_grad, axis=0) / attn_gain

        branch_sum = attn_sum + mlp_sum
        score_grad = jnp.sum(grad_rows * branch_sum, axis=1, keepdims=True)
        router_part = jnp.sum(score_grad * rows, axis=0)
        rows_back = norm_back(rows, inverse_in, attn_gain, normed_grad)
        rows_total = grad_rows + mixed_grad + rows_back + score_grad * router_weight.astype(f32)

        listed = jnp.any(chosen > 0, axis=0)[:, None]
        output = jnp.where(
            listed, dot(chosen, (rows + score * branch_sum).astype(low), ((0,), (0,))).astype(low), tokens
        )
        tokens_grad = jnp.where(
            listed, dot(chosen, rows_total.astype(low), ((0,), (0,))).astype(low), cotangent
        )

        small = jnp.stack([router_part, attn_gain_part, mlp_gain_part])
        for axis, bits in (("dp", dp_bits), ("tensor", [1, 2] + far_bits)):
            for bit in bits:
                small = small + swap(small, axis, bit)

        piece = head_size // dp_size
        cut = qkv_grad.astype(low).reshape(3, shard_count, heads, dp_size, piece, width)
        qkv_out = collect(cut.transpose(1, 3, 0, 2, 4, 5), first)
        qkv_out = qkv_out.transpose(1, 2, 0, 3, 4).reshape(qkv_weight.shape)
        cut = out_grad.astype(low).reshape(shard_count, heads, dp_size, piece, width)
        out_out = collect(cut.transpose(0, 2, 1, 3, 4), second)
        out_out = out_out.transpose(1, 0, 2, 3).reshape(out_weight.shape)
        piece = hidden_own // dp_size
        up_out = collect(up_grad.astype(low).reshape(shard_count, dp_size, piece, width), first)
        up_out = up_out.reshape(hidden_own, width).T
        down_out = collect(down_grad.astype(low).reshape(shard_count, dp_size, piece, width), second)
        down_out = down_out.reshape(hidden_own, width)
        return (
            output,
            tokens_grad,
            small[0],
            small[1],
            qkv_out,
            out_out,
            small[2],
            up_out,
            down_out,
        )

    return local


def solution(mesh):
    rows = P(("dp", "tensor"), None)
    heads = P("tensor", None, None)
    return jax.shard_map(
        make_local(mesh.shape["dp"], mesh.shape["tensor"]),
        mesh=mesh,
        in_specs=(
            rows,
            rows,
            P(),
            P(),
            P(None, "tensor", None, None),
            heads,
            P(),
            P(None, "tensor"),
            P("tensor", None),
            rows,
        ),
        out_specs=(
            rows,
            rows,
            P(),
            P(),
            P(None, "tensor", None, None),
            heads,
            P(),
            P(None, "tensor"),
            P("tensor", None),
        ),
        check_vma=False,
    )
```

time: 613 us -> 333 us (0.54)
  waiting for transfers between devices: 402 us -> 122 us
  starting transfers between devices: 1.24 us -> 61.7 us
  blocking collectives: 38.2 us -> 0 us
  other arithmetic: 54.2 us -> 27.7 us
  local copies, waits for them, and re-layouts: 28.2 us -> 46.9 us
  between operations: 14.8 us -> 1.95 us
    psum x2 -> x0, waiting for transfers between devices: 163 us -> none  [the longest x1 90.7 us: local(): lax.psum(jnp.dot(attended_rows, out_flat, preferred_element_type=jnp.floa...]
    reduce_scatter x3 -> x0, waiting for transfers between devices: 126 us -> none  [the longest x1 48.5 us: local(): lax.psum_scatter(row_product(hidden, down_w).astype(jnp.bfloat16), 'tenso...]
    ppermute x0 -> x69, waiting for transfers between devices: none -> 122 us  [swap(): return lax.ppermute(x, axis, [(i, i ^ bit) for i in range(size)])]
    all_gather x3 -> x0, waiting for transfers between devices: 113 us -> none  [the longest x1 44.8 us: local(): group_rows = lax.all_gather(routed_rows, 'tensor', axis=0, tiled=True)]
    ppermute x0 -> x69, starting transfers between devices: none -> 61.7 us  [swap(): return lax.ppermute(x, axis, [(i, i ^ bit) for i in range(size)])]
    psum x1 -> x0, blocking collectives: 38.2 us -> none  [local(): lax.psum((router_part, attn_gain_part, mlp_gain_part), ('dp', 'tensor'))]
    scatter x2 -> x0, other arithmetic: 15.4 us -> none  [the longest x1 8.02 us: local(): tokens_grad = grad_seqs.at[picker].set(rows_total.astype(jnp.bfloat16).re...]
    unnamed x70 -> x110, local copies, waits for them, and re-layouts: 13.6 us -> 28.5 us
  transfers between devices with their start and end apart: 8 -> 69, of which waited for: 8 -> 25; matrix products, arithmetic and copies ran while one was open for 12% -> 34% of each run, Pallas kernels for 0% -> 0%
where the time goes in v1:
time: 333 us; the launch traced here: 326 us
  waiting for transfers between devices  122 us (37%)
  matrix products  66 us (20%)
  starting transfers between devices  61.7 us (19%)
  local copies, waits for them, and re-layouts  46.9 us (14%)
  other arithmetic  27.7 us (8%)
    ppermute x69, waiting for transfers between devices, swap(): return lax.ppermute(x, axis, [(i, i ^ bit) for i in range(size)])  122 us
    ppermute x69, starting transfers between devices, swap(): return lax.ppermute(x, axis, [(i, i ^ bit) for i in range(size)])  61.7 us
    dot_general x20, matrix products, dot(): lax.dot_general(a, b, (contract, ((), ())), preferred_element_type=f32)  59.7 us
    unnamed x110, local copies, waits for them, and re-layouts  28.5 us
  transfers between devices with their start and end apart: 69, of which 25 were waited for; matrix products, arithmetic and copies ran while one was open for 34% of the time, Pallas kernels for 0%

profile of v1, /device:TPU:0, one launch (start us, length us, event | category | flops | bytes accessed | tf_op | source)
XLA Modules:
  0.0 326.4 jit_solution(9466625613983293121)
XLA Ops:
  1.3 3.6 %multiply_reduce_fusion.8 = (f32[256]{0:T(256)S(1)}, f32[256]{0:T(256)S(1)}, f32[256,1024]{1,0:T(8,128)S(1)}) fusion(f32[1024]{0:T(1024)S(1)} %convert_element_type.379, bf16[2048,1024]{1,0:T(8,128)(2,1)} %param.10, s32[256]{0:T(256)} %bitcast.266), kind=kOutput, calls=%fused_computation.116 | convolution fusion | flops 1075314176 | bytes 5250048 | tf_op jit(solution)/shard_map/dot_general | solution.py:22
  13.9 11.4 %collective-permute-done = bf16[3,2,16,1024]{3,2,1,0:T(8,128)(2,1)} collective-permute-done((bf16[3,2,16,1024]{3,2,1,0:T(8,128)(2,1)S(1)}, bf16[3,2,16,1024]{3,2,1,0:T(8,128)(2,1)}, u32[]{:S(2)}, u32[]{:S(2)}) %collective-permute-start) | collective-permute-done | bytes 196640 | tf_op jit(solution)/shard_map/ppermute | solution.py:31
  37.4 3.5 %collective-permute-start.17 = (bf16[1024,128]{0,1:T(8,128)(2,1)}, bf16[1024,128]{0,1:T(8,128)(2,1)}, u32[]{:S(2)}, u32[]{:S(2)}) collective-permute-start(bf16[1024,128]{0,1:T(8,128)(2,1)} %copy.127), channel_id=1, source_target_pairs={{0,4},{1,5},{2,6},{3,7},{4,0},{5,1},{6,2},{7,3},{8,12},{9,13},{10,... | collective-permute-start | bytes 786440 | tf_op jit(solution)/shard_map/ppermute | solution.py:31
  45.6 3.9 %convolution_convert_fusion.1 = bf16[768,1024]{1,0:T(8,128)(2,1)S(1)} fusion(bf16[768,1024]{1,0:T(8,128)(2,1)S(1)} %bitcast.226, bf16[256,1024]{1,0:T(8,128)(2,1)S(1)} %collective-permute-done.6, bf16[256,1024]{1,0:T(8,128)(2,1)} %collective-permute-done.5, bf16[256,1024]{1,0:T(8,128)(2,1)} %collective-permute-done.4, ...), kind=kOutput, calls=%fused_computation.37 | convolution fusion | flops 1619787776 | bytes 5242880 | tf_op jit(solution)/shard_map/dot_general | solution.py:22
  79.8 8.8 %collective-permute-done.13 = bf16[256,1024]{1,0:T(8,128)(2,1)} collective-permute-done((bf16[256,1024]{1,0:T(8,128)(2,1)}, bf16[256,1024]{1,0:T(8,128)(2,1)}, u32[]{:S(2)}, u32[]{:S(2)}) %collective-permute-start.13) | collective-permute-done | bytes 524320 | tf_op jit(solution)/shard_map/ppermute | solution.py:31
  99.0 4.3 %collective-permute-done.18 = bf16[1024,128]{0,1:T(8,128)(2,1)S(1)} collective-permute-done((bf16[1024,128]{0,1:T(8,128)(2,1)}, bf16[1024,128]{0,1:T(8,128)(2,1)S(1)}, u32[]{:S(2)}, u32[]{:S(2)}) %collective-permute-start.18) | collective-permute-done | bytes 262176 | tf_op jit(solution)/shard_map/ppermute | solution.py:31
  114.1 3.3 collective-permute-done.24
  118.0 5.0 %multiply_convert_fusion.1 = (bf16[1024,1024]{1,0:T(8,128)(2,1)S(1)}, f32[1024,1024]{1,0:T(8,128)S(1)}) fusion(bf16[1024,1024]{0,1:T(8,128)(2,1)} %constant_dynamic-update-slice_fusion, bf16[256,1024]{1,0:T(8,128)(2,1)S(1)} %collective-permute-done.16, bf16[256,1024]{1,0:T(8,128)(2,1)S(1)} %collective-permute-done.15, ...), kind=kOutput, calls=%fused_computation.18 | convolution fusion | flops 2165309440 | bytes 10485760 | tf_op jit(solution)/shard_map/dot_general | solution.py:22
  128.8 8.0 %fusion.9 = bf16[1024,1024]{1,0:T(8,128)(2,1)S(1)} fusion(f32[1024,1024]{1,0:T(8,128)S(1)} %get-tuple-element.83, bf16[1024,1024]{1,0:T(8,128)(2,1)} %constant_dynamic-update-slice_fusion.8, bf16[256,1024]{1,0:T(8,128)(2,1)S(1)} %collective-permute-done.30, bf16[256,1024]{1,0:T(8,128)(2,1)S(1)} %collective-permute-done.29, ...), kind=kOutput, calls=%fused_computation.11 | convolution fusion | flops 2175795200 | bytes 10485760 | tf_op jit(solution)/shard_map/dot_general | solution.py:22
  139.6 4.5 %fusion.98 = (bf16[1024,1024]{1,0:T(8,128)(2,1)S(1)}, f32[1024]{0:T(1024)S(1)}) fusion(bf16[1024,1024]{0,1:T(8,128)(2,1)} %constant_dynamic-update-slice_fusion, bf16[1024,1024]{1,0:T(8,128)(2,1)S(1)} %fusion.9, bf16[256,1024]{1,0:T(8,128)(2,1)S(1)} %collective-permute-done.16, bf16[256,1024]{1,0:T(8,128)(2,1)S(1)} %collective-permute-done.15, ...), kind=kOutput, calls=%fused_computation.251 | convolution fusion | flops 2160065536 | bytes 8392704 | tf_op jit(solution)/shard_map/dot_general | solution.py:22
  145.4 3.6 %convolution_convert_fusion = bf16[1024,1024]{1,0:T(8,128)(2,1)S(1)} fusion(bf16[1024,1024]{1,0:T(8,128)(2,1)S(1)} %get-tuple-element.82, bf16[256,1024]{1,0:T(8,128)(2,1)S(1)} %collective-permute-done.30, bf16[256,1024]{1,0:T(8,128)(2,1)S(1)} %collective-permute-done.29, bf16[256,1024]{1,0:T(8,128)(2,1)} %collective-permute-done.28, ...), kind=kOutput, calls=%fused_computation.36 | convolution fusion | flops 2156920832 | bytes 6291456 | tf_op jit(solution)/shard_map/dot_general | solution.py:22
  155.0 12.3 %collective-permute-done.57 = bf16[2,2,128,1024]{3,2,1,0:T(8,128)(2,1)S(1)} collective-permute-done((bf16[2,2,128,1024]{3,2,1,0:T(8,128)(2,1)S(1)}, bf16[2,2,128,1024]{3,2,1,0:T(8,128)(2,1)S(1)}, u32[]{:S(2)}, u32[]{:S(2)}) %collective-permute-start.57) | collective-permute-done | bytes 1048608 | tf_op jit(solution)/shard_map/ppermute | solution.py:31
  167.7 4.9 %collective-permute-done.63 = bf16[2,2,128,1024]{3,2,1,0:T(8,128)(2,1)S(1)} collective-permute-done((bf16[2,2,128,1024]{3,2,1,0:T(8,128)(2,1)S(1)}, bf16[2,2,128,1024]{3,2,1,0:T(8,128)(2,1)S(1)}, u32[]{:S(2)}, u32[]{:S(2)}) %collective-permute-start.63) | collective-permute-done | bytes 1048608 | tf_op jit(solution)/shard_map/ppermute | solution.py:31
  174.8 4.8 %collective-permute-done.33 = bf16[256,1024]{1,0:T(8,128)(2,1)S(1)} collective-permute-done((bf16[256,1024]{1,0:T(8,128)(2,1)S(1)}, bf16[256,1024]{1,0:T(8,128)(2,1)S(1)}, u32[]{:S(2)}, u32[]{:S(2)}) %collective-permute-start.33) | collective-permute-done | bytes 524320 | tf_op jit(solution)/shard_map/ppermute | solution.py:31
  187.0 14.7 %collective-permute-done.34 = bf16[256,1024]{1,0:T(8,128)(2,1)S(1)} collective-permute-done((bf16[256,1024]{1,0:T(8,128)(2,1)S(1)}, bf16[256,1024]{1,0:T(8,128)(2,1)S(1)}, u32[]{:S(2)}, u32[]{:S(2)}) %collective-permute-start.34) | collective-permute-done | bytes 524320 | tf_op jit(solution)/shard_map/ppermute | solution.py:31
  201.7 3.5 %convert_select_fusion.1 = bf16[2048,1024]{1,0:T(8,128)(2,1)} fusion(bf16[2048,1024]{1,0:T(8,128)(2,1)S(1)} %copy-done.36, pred[2048]{0:T(1024)(128)(4,1)S(1)} %compare_reduce_fusion, s32[256]{0:T(256)S(1)} %bitcast.269, f32[256,1024]{1,0:T(8,128)S(1)} %get-tuple-element.77, f32[256,1024]{1,0:T(8,128)S(1)} %get-tuple-element.45, f32[256]{0:T(256)S(1)} %get-tuple-element.11), kind=kOutput, calls=%fused_computation.17 | convolution fusion | flops 1079246848 | bytes 10489856 | tf_op jit(solution)/shard_map/dot_general | solution.py:22
  238.7 5.0 %collective-permute-done.62 = bf16[128,1024]{1,0:T(8,128)(2,1)S(1)} collective-permute-done((bf16[128,1024]{1,0:T(8,128)(2,1)S(1)}, bf16[128,1024]{1,0:T(8,128)(2,1)S(1)}, u32[]{:S(2)}, u32[]{:S(2)}) %collective-permute-start.62) | collective-permute-done | bytes 262176 | tf_op jit(solution)/shard_map/ppermute | solution.py:31
  247.3 14.0 %collective-permute-done.52 = bf16[1,2,2,16,1024]{4,3,2,1,0:T(8,128)(2,1)S(1)} collective-permute-done((bf16[1,2,2,16,1024]{4,3,2,1,0:T(8,128)(2,1)S(1)}, bf16[1,2,2,16,1024]{4,3,2,1,0:T(8,128)(2,1)S(1)}, u32[]{:S(2)}, u32[]{:S(2)}) %collective-permute-start.52) | collective-permute-done | bytes 131104 | tf_op jit(solution)/shard_map/ppermute | solution.py:31
  263.1 3.5 %collective-permute-done.53 = bf16[1,2,16,1024]{3,2,1,0:T(8,128)(2,1)S(1)} collective-permute-done((bf16[1,2,16,1024]{3,2,1,0:T(8,128)(2,1)S(1)}, bf16[1,2,16,1024]{3,2,1,0:T(8,128)(2,1)S(1)}, u32[]{:S(2)}, u32[]{:S(2)}) %collective-permute-start.53) | collective-permute-done | bytes 65568 | tf_op jit(solution)/shard_map/ppermute | solution.py:31
  275.3 4.5 %collective-permute-done.39 = bf16[256,1024]{1,0:T(8,128)(2,1)} collective-permute-done((bf16[256,1024]{1,0:T(8,128)(2,1)}, bf16[256,1024]{1,0:T(8,128)(2,1)}, u32[]{:S(2)}, u32[]{:S(2)}) %collective-permute-start.39) | collective-permute-done | bytes 524320 | tf_op jit(solution)/shard_map/ppermute | solution.py:31
  286.6 5.6 %collective-permute-done.41 = f32[3,1024]{1,0:T(4,128)S(1)} collective-permute-done((f32[3,1024]{1,0:T(4,128)S(1)}, f32[3,1024]{1,0:T(4,128)S(1)}, u32[]{:S(2)}, u32[]{:S(2)}) %collective-permute-start.41) | collective-permute-done | bytes 12320 | tf_op jit(solution)/shard_map/ppermute | solution.py:31
  298.0 9.9 %collective-permute-done.47 = bf16[1,3,2,16,1024]{4,3,2,0,1:T(8,128)(2,1)S(1)} collective-permute-done((bf16[1,3,2,16,1024]{4,3,2,0,1:T(8,128)(2,1)S(1)}, bf16[1,3,2,16,1024]{4,3,2,0,1:T(8,128)(2,1)S(1)}, u32[]{:S(2)}, u32[]{:S(2)}) %collective-permute-start.47) | collective-permute-done | bytes 196640 | tf_op jit(solution)/shard_map/ppermute | solution.py:31
  309.0 5.3 %convert_select_fusion = bf16[2048,1024]{1,0:T(8,128)(2,1)} fusion(bf16[2048,1024]{1,0:T(8,128)(2,1)S(1)} %copy-done.3, pred[2048]{0:T(1024)(128)(4,1)S(1)} %compare_reduce_fusion, s32[256]{0:T(256)S(1)} %bitcast.270, f32[256,1024]{1,0:T(8,128)S(1)} %copy-done.9, f32[256,1024]{1,0:T(8,128)S(1)} %copy-done.10, f32[256,1024]{1,0:T(8,128)S(1)} %get-tuple-element.77, ...), kind=kOutput, calls=%fused_computation.14 | convolution fusion | flops 1082130432 | bytes 13645824 | tf_op jit(solution)/shard_map/dot_general | solution.py:22
  316.9 5.2 %collective-permute-done.48 = bf16[3,2,16,1024]{3,2,1,0:T(8,128)(2,1)S(1)} collective-permute-done((bf16[3,2,16,1024]{3,2,1,0:T(8,128)(2,1)S(1)}, bf16[3,2,16,1024]{3,2,1,0:T(8,128)(2,1)S(1)}, u32[]{:S(2)}, u32[]{:S(2)}) %collective-permute-start.48) | collective-permute-done | bytes 196640 | tf_op jit(solution)/shard_map/ppermute | solution.py:31
  (337 shorter events, 171.4 us)
Async XLA Ops:
  6.0 30.8 %collective-permute-start.4 = (bf16[256,1024]{1,0:T(8,128)(2,1)}, bf16[256,1024]{1,0:T(8,128)(2,1)}, u32[]{:S(2)}, u32[]{:S(2)}) collective-permute-start(bf16[256,1024]{1,0:T(8,128)(2,1)} %multiply_convert_fusion.3), channel_id=1, source_target_pairs={{0,2},{1,3},{2,0},{3,1},{4,6},{5,7},{6,4},{7,5},{8,10},{9,11},{10,... | collective-permute-start | bytes 1572872 | tf_op jit(solution)/shard_map/ppermute | solution.py:31
  12.9 32.7 %collective-permute-start.5 = (bf16[256,1024]{1,0:T(8,128)(2,1)}, bf16[256,1024]{1,0:T(8,128)(2,1)}, u32[]{:S(2)}, u32[]{:S(2)}) collective-permute-start(bf16[256,1024]{1,0:T(8,128)(2,1)} %multiply_convert_fusion.3), channel_id=1, source_target_pairs={{0,1},{1,0},{2,3},{3,2},{4,5},{5,4},{6,7},{7,6},{8,9},{9,8},{10,11... | collective-permute-start | bytes 1572872 | tf_op jit(solution)/shard_map/ppermute | solution.py:31
  37.4 56.5 %collective-permute-start.17 = (bf16[1024,128]{0,1:T(8,128)(2,1)}, bf16[1024,128]{0,1:T(8,128)(2,1)}, u32[]{:S(2)}, u32[]{:S(2)}) collective-permute-start(bf16[1024,128]{0,1:T(8,128)(2,1)} %copy.127), channel_id=1, source_target_pairs={{0,4},{1,5},{2,6},{3,7},{4,0},{5,1},{6,2},{7,3},{8,12},{9,13},{10,... | collective-permute-start | bytes 786440 | tf_op jit(solution)/shard_map/ppermute | solution.py:31
  41.9 54.3 %collective-permute-start.21 = (bf16[128,1024]{1,0:T(8,128)(2,1)}, bf16[128,1024]{1,0:T(8,128)(2,1)}, u32[]{:S(2)}, u32[]{:S(2)}) collective-permute-start(bf16[128,1024]{1,0:T(8,128)(2,1)} %get-tuple-element.20), channel_id=1, source_target_pairs={{0,4},{1,5},{2,6},{3,7},{4,0},{5,1},{6,2},{7,3},{8,12},{9,13},{10,... | collective-permute-start | bytes 786440 | tf_op jit(solution)/shard_map/ppermute | solution.py:31
  63.2 49.6 %collective-permute-start.28 = (bf16[256,1024]{1,0:T(8,128)(2,1)}, bf16[256,1024]{1,0:T(8,128)(2,1)}, u32[]{:S(2)}, u32[]{:S(2)}) collective-permute-start(bf16[256,1024]{1,0:T(8,128)(2,1)} %get-tuple-element.80), channel_id=1, source_target_pairs={{0,2},{1,3},{2,0},{3,1},{4,6},{5,7},{6,4},{7,5},{8,10},{9,11},{10,... | collective-permute-start | bytes 1572872 | tf_op jit(solution)/shard_map/ppermute | solution.py:31
  69.9 18.6 %collective-permute-start.13 = (bf16[256,1024]{1,0:T(8,128)(2,1)}, bf16[256,1024]{1,0:T(8,128)(2,1)}, u32[]{:S(2)}, u32[]{:S(2)}) collective-permute-start(bf16[256,1024]{1,0:T(8,128)(2,1)} %fusion.39), channel_id=1, source_target_pairs={{0,2},{1,3},{2,0},{3,1},{4,6},{5,7},{6,4},{7,5},{8,10},{9,11},{10,... | collective-permute-start | bytes 1572872 | tf_op jit(solution)/shard_map/ppermute | solution.py:31
  144.3 23.0 %collective-permute-start.57 = (bf16[2,2,128,1024]{3,2,1,0:T(8,128)(2,1)S(1)}, bf16[2,2,128,1024]{3,2,1,0:T(8,128)(2,1)S(1)}, u32[]{:S(2)}, u32[]{:S(2)}) collective-permute-start(bf16[2,2,128,1024]{3,2,1,0:T(8,128)(2,1)S(1)} %pad_maximum_fusion.5), channel_id=1, source_target_pairs={{0,8},{8,0},{16,24},{24,16},{1,9},{9,1},{17,25},{25,17},{2,10},{10... | collective-permute-start | bytes 3145736 | tf_op jit(solution)/shard_map/ppermute | solution.py:31
  149.2 23.4 %collective-permute-start.63 = (bf16[2,2,128,1024]{3,2,1,0:T(8,128)(2,1)S(1)}, bf16[2,2,128,1024]{3,2,1,0:T(8,128)(2,1)S(1)}, u32[]{:S(2)}, u32[]{:S(2)}) collective-permute-start(bf16[2,2,128,1024]{3,2,1,0:T(8,128)(2,1)S(1)} %pad_maximum_fusion.8), channel_id=1, source_target_pairs={{0,16},{8,24},{16,0},{24,8},{1,17},{9,25},{17,1},{25,9},{2,18},{10... | collective-permute-start | bytes 3145736 | tf_op jit(solution)/shard_map/ppermute | solution.py:31
  150.2 29.8 %collective-permute-start.25 = (bf16[256,1024]{1,0:T(8,128)(2,1)S(1)}, bf16[256,1024]{1,0:T(8,128)(2,1)S(1)}, u32[]{:S(2)}, u32[]{:S(2)}) collective-permute-start(bf16[256,1024]{1,0:T(8,128)(2,1)S(1)} %get-tuple-element.48), channel_id=1, source_target_pairs={{0,1},{1,0},{2,3},{3,2},{4,5},{5,4},{6,7},{7,6},{8,9},{9,8},{10,11... | collective-permute-start | bytes 1572872 | tf_op jit(solution)/shard_map/ppermute | solution.py:31
  153.8 19.8 %collective-permute-start.31 = (bf16[256,1024]{1,0:T(8,128)(2,1)S(1)}, bf16[256,1024]{1,0:T(8,128)(2,1)S(1)}, u32[]{:S(2)}, u32[]{:S(2)}) collective-permute-start(bf16[256,1024]{1,0:T(8,128)(2,1)S(1)} %get-tuple-element.46), channel_id=1, source_target_pairs={{0,1},{1,0},{2,3},{3,2},{4,5},{5,4},{6,7},{7,6},{8,9},{9,8},{10,11... | collective-permute-start | bytes 1572872 | tf_op jit(solution)/shard_map/ppermute | solution.py:31
  154.5 25.6 %collective-permute-start.27 = (bf16[256,1024]{1,0:T(8,128)(2,1)S(1)}, bf16[256,1024]{1,0:T(8,128)(2,1)S(1)}, u32[]{:S(2)}, u32[]{:S(2)}) collective-permute-start(bf16[256,1024]{1,0:T(8,128)(2,1)S(1)} %fusion.33), channel_id=1, source_target_pairs={{0,2},{1,3},{2,0},{3,1},{4,6},{5,7},{6,4},{7,5},{8,10},{9,11},{10,... | collective-permute-start | bytes 1572872 | tf_op jit(solution)/shard_map/ppermute | solution.py:31
  183.0 18.7 %collective-permute-start.34 = (bf16[256,1024]{1,0:T(8,128)(2,1)S(1)}, bf16[256,1024]{1,0:T(8,128)(2,1)S(1)}, u32[]{:S(2)}, u32[]{:S(2)}) collective-permute-start(bf16[256,1024]{1,0:T(8,128)(2,1)S(1)} %get-tuple-element.13), channel_id=1, source_target_pairs={{0,2},{1,3},{2,0},{3,1},{4,6},{5,7},{6,4},{7,5},{8,10},{9,11},{10,... | collective-permute-start | bytes 1572872 | tf_op jit(solution)/shard_map/ppermute | solution.py:31
  183.3 28.2 %collective-permute-start.35 = (bf16[256,1024]{1,0:T(8,128)(2,1)S(1)}, bf16[256,1024]{1,0:T(8,128)(2,1)S(1)}, u32[]{:S(2)}, u32[]{:S(2)}) collective-permute-start(bf16[256,1024]{1,0:T(8,128)(2,1)S(1)} %get-tuple-element.13), channel_id=1, source_target_pairs={{0,1},{1,0},{2,3},{3,2},{4,5},{5,4},{6,7},{7,6},{8,9},{9,8},{10,11... | collective-permute-start | bytes 1572872 | tf_op jit(solution)/shard_map/ppermute | solution.py:31
  183.6 21.6 %collective-permute-start.59 = (bf16[1,128,1024]{2,1,0:T(8,128)(2,1)S(1)}, bf16[1,128,1024]{2,1,0:T(8,128)(2,1)S(1)}, u32[]{:S(2)}, u32[]{:S(2)}) collective-permute-start(bf16[1,128,1024]{2,1,0:T(8,128)(2,1)S(1)} %slice.304), channel_id=1, source_target_pairs={{0,4},{1,5},{2,6},{3,7},{4,0},{5,1},{6,2},{7,3},{8,12},{9,13},{10,... | collective-permute-start | bytes 786440 | tf_op jit(solution)/shard_map/ppermute | solution.py:31
  185.6 24.6 %collective-permute-start.65 = (bf16[1,128,1024]{2,1,0:T(8,128)(2,1)S(1)}, bf16[1,128,1024]{2,1,0:T(8,128)(2,1)S(1)}, u32[]{:S(2)}, u32[]{:S(2)}) collective-permute-start(bf16[1,128,1024]{2,1,0:T(8,128)(2,1)S(1)} %slice.312), channel_id=1, source_target_pairs={{0,4},{1,5},{2,6},{3,7},{4,0},{5,1},{6,2},{7,3},{8,12},{9,13},{10,... | collective-permute-start | bytes 786440 | tf_op jit(solution)/shard_map/ppermute | solution.py:31
  205.3 29.1 %collective-permute-start.61 = (bf16[128,1024]{1,0:T(8,128)(2,1)S(1)}, bf16[128,1024]{1,0:T(8,128)(2,1)S(1)}, u32[]{:S(2)}, u32[]{:S(2)}) collective-permute-start(bf16[128,1024]{1,0:T(8,128)(2,1)S(1)} %bitcast.236), channel_id=1, source_target_pairs={{0,16},{8,24},{16,0},{24,8},{1,17},{9,25},{17,1},{25,9},{2,18},{10... | collective-permute-start | bytes 786440 | tf_op jit(solution)/shard_map/ppermute | solution.py:31
  206.8 31.8 %collective-permute-start.60 = (bf16[128,1024]{1,0:T(8,128)(2,1)S(1)}, bf16[128,1024]{1,0:T(8,128)(2,1)}, u32[]{:S(2)}, u32[]{:S(2)}) collective-permute-start(bf16[128,1024]{1,0:T(8,128)(2,1)S(1)} %bitcast.237), channel_id=1, source_target_pairs={{0,8},{8,0},{16,24},{24,16},{1,9},{9,1},{17,25},{25,17},{2,10},{10... | collective-permute-start | bytes 786440 | tf_op jit(solution)/shard_map/ppermute | solution.py:31
  210.3 26.0 %collective-permute-start.66 = (bf16[128,1024]{1,0:T(8,128)(2,1)S(1)}, bf16[128,1024]{1,0:T(8,128)(2,1)}, u32[]{:S(2)}, u32[]{:S(2)}) collective-permute-start(bf16[128,1024]{1,0:T(8,128)(2,1)S(1)} %bitcast.238), channel_id=1, source_target_pairs={{0,8},{8,0},{16,24},{24,16},{1,9},{9,1},{17,25},{25,17},{2,10},{10... | collective-permute-start | bytes 786440 | tf_op jit(solution)/shard_map/ppermute | solution.py:31
  211.5 33.3 %collective-permute-start.67 = (bf16[128,1024]{1,0:T(8,128)(2,1)S(1)}, bf16[128,1024]{1,0:T(8,128)(2,1)}, u32[]{:S(2)}, u32[]{:S(2)}) collective-permute-start(bf16[128,1024]{1,0:T(8,128)(2,1)S(1)} %bitcast.239), channel_id=1, source_target_pairs={{0,16},{8,24},{16,0},{24,8},{1,17},{9,25},{17,1},{25,9},{2,18},{10... | collective-permute-start | bytes 786440 | tf_op jit(solution)/shard_map/ppermute | solution.py:31
  236.3 46.5 %collective-permute-start.45 = (bf16[2,2,3,2,16,1024]{5,4,3,1,2,0:T(8,128)(2,1)}, bf16[2,2,3,2,16,1024]{5,4,3,1,2,0:T(8,128)(2,1)}, u32[]{:S(2)}, u32[]{:S(2)}) collective-permute-start(bf16[2,2,3,2,16,1024]{5,4,3,1,2,0:T(8,128)(2,1)} %pad_maximum_fusion.11), channel_id=1, source_target_pairs={{0,8},{8,0},{16,24},{24,16},{1,9},{9,1},{17,25},{25,17},{2,10},{10... | collective-permute-start | bytes 2359304 | tf_op jit(solution)/shard_map/ppermute | solution.py:31
  238.7 29.1 %collective-permute-start.38 = (bf16[256,1024]{1,0:T(8,128)(2,1)S(1)}, bf16[256,1024]{1,0:T(8,128)(2,1)S(1)}, u32[]{:S(2)}, u32[]{:S(2)}) collective-permute-start(bf16[256,1024]{1,0:T(8,128)(2,1)S(1)} %get-tuple-element.43), channel_id=1, source_target_pairs={{0,1},{1,0},{2,3},{3,2},{4,5},{5,4},{6,7},{7,6},{8,9},{9,8},{10,11... | collective-permute-start | bytes 1572872 | tf_op jit(solution)/shard_map/ppermute | solution.py:31
  243.7 31.6 %collective-permute-start.37 = (bf16[256,1024]{1,0:T(8,128)(2,1)}, bf16[256,1024]{1,0:T(8,128)(2,1)}, u32[]{:S(2)}, u32[]{:S(2)}) collective-permute-start(bf16[256,1024]{1,0:T(8,128)(2,1)} %get-tuple-element.42), channel_id=1, source_target_pairs={{0,1},{1,0},{2,3},{3,2},{4,5},{5,4},{6,7},{7,6},{8,9},{9,8},{10,11... | collective-permute-start | bytes 1572872 | tf_op jit(solution)/shard_map/ppermute | solution.py:31
  244.8 16.5 %collective-permute-start.52 = (bf16[1,2,2,16,1024]{4,3,2,1,0:T(8,128)(2,1)S(1)}, bf16[1,2,2,16,1024]{4,3,2,1,0:T(8,128)(2,1)S(1)}, u32[]{:S(2)}, u32[]{:S(2)}) collective-permute-start(bf16[1,2,2,16,1024]{4,3,2,1,0:T(8,128)(2,1)S(1)} %fusion.83), channel_id=1, source_target_pairs={{0,8},{8,0},{16,24},{24,16},{1,9},{9,1},{17,25},{25,17},{2,10},{10... | collective-permute-start | bytes 393224 | tf_op jit(solution)/shard_map/ppermute | solution.py:31
  297.2 17.0 %collective-permute-start.44 = (f32[3,1024]{1,0:T(4,128)S(1)}, f32[3,1024]{1,0:T(4,128)S(1)}, u32[]{:S(2)}, u32[]{:S(2)}) collective-permute-start(f32[3,1024]{1,0:T(4,128)S(1)} %add.245), channel_id=1, source_target_pairs={{0,4},{1,5},{2,6},{3,7},{4,0},{5,1},{6,2},{7,3},{8,12},{9,13},{10,... | collective-permute-start | bytes 36872 | tf_op jit(solution)/shard_map/ppermute | solution.py:31
  (90 other events, 770.9 us)
